TPU v7x, 32 devices: a whole 2x2x4 slice. The times are simulated.
32 devices in a mesh: dp: 8 (over y, x, core), tensor: 4 (over z).
Axes of the slice: x: 2, y: 2, z: 4, core: 2. Of those that a mesh axis runs over, the one named last changes fastest.
Arguments:
- out_grad: bfloat16 [16384, 512], P('dp'), may hold values from -0.0625 to 0.0625
- inputs: bfloat16 [16384, 8192], P('dp', 'tensor'), may hold values from -6 to 6
- weights: float32 [512, 8192], P('dp', 'tensor'), may hold values from -60 to 60
- moment: float32 [512, 8192], P('dp', 'tensor'), may hold values from -3 to 3
- second: float32 [512, 8192], P('dp', 'tensor'), may hold values from 0.05 to 2
Outputs:
- new_weights: float32 [512, 8192], P('dp', 'tensor')
- new_moment: float32 [512, 8192], P('dp', 'tensor')
- new_second: float32 [512, 8192], P('dp', 'tensor')
All inputs are finite; a program needn't handle non-finite values.
Results may differ from a plain program's by a relative error of at most 0.0003.
Values sent between devices are 32-bit elements; how exact they have to be, the bound alone decides.
A program may use at most 128 MiB of HBM per device.

v0:
```python
import jax
import jax.numpy as jnp
from jax import lax
from jax.sharding import PartitionSpec as P


def finish(grad, weights, moment, second):
    new_moment = 0.9 * moment + 0.1 * grad
    new_second = 0.95 * second + 0.05 * grad * grad
    step_size = 0.3 * (new_moment / (1.0 - 0.9**10))
    moved = weights - step_size / (jnp.sqrt(new_second / (1.0 - 0.95**10)) + 1e-08)
    return (moved, new_moment, new_second)


def rescale(moved, totals, width):
    mean_square = totals[:, None] / width
    return moved / jnp.sqrt(mean_square + 1e-06)


def on_device(out_grad, inputs, weights, moment, second):
    width = weights.shape[1] * lax.axis_size("tensor")
    grad = lax.psum_scatter(
        lax.dot_general(
            out_grad, inputs, (((0,), (0,)), ((), ())), preferred_element_type=jnp.float32
        ),
        "dp",
        scatter_dimension=0,
        tiled=True,
    )
    moved, new_moment, new_second = finish(grad, weights, moment, second)
    totals = lax.psum(jnp.sum(moved * moved, axis=1), "tensor")
    return (rescale(moved, totals, width), new_moment, new_second)


def solution(mesh):
    in_specs = (
        P("dp", None),
        P("dp", "tensor"),
        P("dp", "tensor"),
        P("dp", "tensor"),
        P("dp", "tensor"),
    )
    out_specs = (P("dp", "tensor"), P("dp", "tensor"), P("dp", "tensor"))
    return jax.shard_map(
        on_device, mesh=mesh, in_specs=in_specs, out_specs=out_specs, check_vma=False
    )
```

profile of v0, /device:TPU:0, one launch (start us, length us, event | category | flops | bytes accessed | tf_op | source)
XLA Modules:
  0.0 94.6 jit_solution(6476871303375612717)
XLA Ops:
  7.2 0.0 copy-start
  7.2 0.0 reduce-scatter.2.cloned.1.call-start
  7.2 1.5 %copy-done = bf16[2048,512]{1,0:T(8,128)(2,1)S(1)} copy-done((bf16[2048,512]{1,0:T(8,128)(2,1)S(1)}, bf16[2048,512]{1,0:T(8,128)(2,1)}, u32[]{:S(2)}) %copy-start) | copy-done | bytes 2097176
  8.8 9.4 %fusion.2 = f32[512,2048]{1,0:T(8,128)} fusion(bf16[2048,512]{1,0:T(8,128)(2,1)S(1)} %copy-done, bf16[2048,2048]{1,0:T(8,128)(2,1)} %param.6), kind=kOutput, calls=%fused_computation.7 | convolution fusion | flops 4294967296 | bytes 14680064 | tf_op jit(solution)/shard_map/dot_general | solution.py:23
  18.2 0.0 copy-start.1
  18.2 0.0 reduce-scatter.2.cloned.1.call-update
  18.2 54.2 %reduce-scatter.2.cloned.1.call-done = f32[64,2048]{1,0:T(8,128)} async-done(((f32[512,2048]{1,0:T(8,128)}), f32[64,2048]{1,0:T(8,128)}) %reduce-scatter.2.cloned.1.call-update) | async-done | bytes 524304 | tf_op jit(solution)/shard_map/reduce_scatter | solution.py:22
  72.4 0.0 copy-done.1
  72.4 2.8 %multiply_reduce_fusion = (f32[64]{0:T(128)S(1)}, f32[64,2048]{1,0:T(8,128)S(1)}, f32[64,2048]{1,0:T(8,128)}, f32[64,2048]{1,0:T(8,128)}) fusion(f32[64,2048]{1,0:T(8,128)S(1)} %copy-done.1, f32[64,2048]{1,0:T(8,128)} %reduce-scatter.2.cloned.1.call-done, f32[64,2048]{1,0:T(8,128)} %param.8, f32[64,2048]{1,0:T(8,128)} %param.9), kind=kLoop, calls=%fused_computation.2 | loop fusion | flops 1834944 | bytes 3670272 | tf_op jit(solution)/shard_map/reduce_sum | solution.py:31
  75.2 11.7 %psum.7 = f32[64]{0:T(128)S(1)} all-reduce(f32[64]{0:T(128)S(1)} %get-tuple-element.3), channel_id=1, replica_groups=mesh['dp'=8,'tensor'=4] {'tensor'}, use_global_device_ids=true, to_apply=%region_2.0 | all-reduce | flops 64 | bytes 512 | tf_op jit(solution)/shard_map/psum | solution.py:31
  86.9 0.9 broadcast_divide_fusion
  (1 shorter events, 0.0 us)
Async XLA Ops:
  7.2 1.6 %copy-start = (bf16[2048,512]{1,0:T(8,128)(2,1)S(1)}, bf16[2048,512]{1,0:T(8,128)(2,1)}, u32[]{:S(2)}) copy-start(bf16[2048,512]{1,0:T(8,128)(2,1)} %param.5) | copy-start | bytes 6291460
  7.2 65.2 %reduce-scatter.2.cloned.1.call-start = ((), (), s32[]{:S(2)}) async-start(), calls=%async_computation.1 | async-start | bytes 4718592 | tf_op jit(solution)/shard_map/reduce_scatter | solution.py:22
  18.2 54.2 %copy-start.1 = (f32[64,2048]{1,0:T(8,128)S(1)}, f32[64,2048]{1,0:T(8,128)}, u32[]{:S(2)}) copy-start(f32[64,2048]{1,0:T(8,128)} %param.7) | copy-start | bytes 1572868
Sparse Core Ops, SparseCore 0:
  18.3 53.9 reduce-scatter.1
where the time goes:
time: 94.9 us; the launch traced here: 94.6 us
  waiting for transfers between devices  54.2 us (57%)
  between operations  14 us (15%)
  blocking collectives  11.7 us (12%)
  matrix products  9.42 us (10%)
  other arithmetic  3.71 us (4%)
  local copies, waits for them, and re-layouts  1.55 us (2%)
    reduce_scatter x1, waiting for transfers between devices, on_device(): lax.psum_scatter(lax.dot_general(out_grad, inputs, (((0,), (0,)), ((), ()...  54.2 us
    psum x1, blocking collectives, on_device(): totals = lax.psum(jnp.sum(moved * moved, axis=1), 'tensor')  11.7 us
    dot_general x1, matrix products, on_device(): lax.dot_general(out_grad, inputs, (((0,), (0,)), ((), ())), preferred_ele...  9.42 us
    reduce_sum x1, other arithmetic, on_device(): totals = lax.psum(jnp.sum(moved * moved, axis=1), 'tensor')  2.79 us
  transfers between devices with their start and end apart: 1, of which 1 were waited for; matrix products, arithmetic and copies ran while one was open for 0% of the time, Pallas kernels for 0%

commit v1 on v0

v1 whole, which is shorter than its diff:
```python
import functools

import jax
import jax.numpy as jnp
from jax import lax
from jax.experimental import pallas as pl
from jax.experimental.pallas import tpu as pltpu
from jax.sharding import PartitionSpec as P

MESH = pl.DeviceIdType.MESH
CHUNK = 256
SLOTS = 4
GROUP = 512
LAG = 3


def finish(grad, weights, moment, second):
    new_moment = 0.9 * moment + 0.1 * grad
    new_second = 0.95 * second + 0.05 * grad * grad
    step_size = 0.3 * (new_moment / (1.0 - 0.9**10))
    moved = weights - step_size / (jnp.sqrt(new_second / (1.0 - 0.95**10)) + 1e-08)
    return (moved, new_moment, new_second)


def bit(index, b):
    return lax.rem(index // (1 << b), 2)


def kernel(
    dp, nt, og_hbm, in_hbm, w_hbm, m_hbm, s_hbm, out_w, out_m, out_s, *scratch
):
    bits = dp.bit_length() - 1
    og, og_t, ins, wms, res, acc, tot, zsend, zrecv = scratch[:9]
    recv = scratch[9 : 9 + bits]
    og_sem, in_sem, wms_sem, out_sem, send_sem, recv_sem, zs_sem, zr_sem = scratch[9 + bits :]
    tokens, rows = og.shape
    block = rows // dp
    width = w_hbm.shape[1]
    n = width // CHUNK
    me, z = lax.axis_index("dp"), lax.axis_index("tensor")

    plane = (bits - 1) // 2
    along_x = list(range(1, 1 + plane))
    along_y = list(range(1 + plane, bits))
    orders = ([0] + along_x + along_y, [0] + along_y + along_x)

    def partner(b):
        mine = bit(me, b)
        return (me + (1 - 2 * mine) * (1 << b), z)

    def cols(j):
        return slice(j * CHUNK, (j + 1) * CHUNK)

    def in_copy(j):
        return pltpu.make_async_copy(
            in_hbm.at[:, cols(j)], ins.at[j % SLOTS], in_sem.at[j % SLOTS]
        )

    def exchange(s, j):
        half = dp >> (s + 1)
        return pltpu.make_async_remote_copy(
            src_ref=acc.at[j, pl.ds(half, half)],
            dst_ref=recv[s].at[j],
            send_sem=send_sem.at[s, j],
            recv_sem=recv_sem.at[s, j],
            device_id=partner(orders[j % 2][s]),
            device_id_type=MESH,
        )

    og_copy = pltpu.make_async_copy(og_hbm, og, og_sem)
    og_copy.start()
    for j in range(min(SLOTS, n)):
        in_copy(j).start()
    wms_copies = [
        pltpu.make_async_copy(ref, wms.at[i], wms_sem.at[i])
        for i, ref in enumerate((w_hbm, m_hbm, s_hbm))
    ]
    for copy in wms_copies:
        copy.start()

    barrier = pltpu.get_barrier_semaphore()
    peers = [lax.rem(z + d, nt) for d in range(1, nt)]
    for b in range(bits):
        pl.semaphore_signal(barrier, inc=1, device_id=partner(b), device_id_type=MESH)
    for peer in peers:
        pl.semaphore_signal(barrier, inc=1, device_id=(me, peer), device_id_type=MESH)

    tile = 256
    eye = (
        lax.broadcasted_iota(jnp.int32, (tile, tile), 0)
        == lax.broadcasted_iota(jnp.int32, (tile, tile), 1)
    ).astype(jnp.bfloat16)
    og_copy.wait()

    @pl.loop(0, rows // tile)
    def _(r):
        at = pl.ds(pl.multiple_of(r * tile, tile), tile)
        for k in range(tokens // tile):
            ks = slice(k * tile, (k + 1) * tile)
            og_t[at, ks] = lax.dot_general(
                eye, og[ks, at], (((1,), (1,)), ((), ())), preferred_element_type=jnp.float32
            ).astype(jnp.bfloat16)

    def multiply(j):
        in_copy(j).wait()

        def group(g, _):
            at = pl.ds(pl.multiple_of(g * GROUP, GROUP), GROUP)
            part = jnp.dot(
                og_t[at, :], ins[j % SLOTS], preferred_element_type=jnp.float32
            )
            for o in range(GROUP // block):
                owner = g * (GROUP // block) + o
                place = 0
                for s, b in enumerate(orders[j % 2]):
                    place += lax.rem(bit(me, b) + bit(owner, b), 2) * (dp >> (s + 1))
                acc[j, place] = part[o * block : (o + 1) * block]
            return 0

        lax.fori_loop(0, rows // GROUP, group, 0)
        if j + SLOTS < n:
            in_copy(j + SLOTS).start()

    def out_copies(j):
        return [
            pltpu.make_async_copy(
                res.at[i, :, cols(j)], ref.at[:, cols(j)], out_sem.at[i, j]
            )
            for i, ref in enumerate((out_w, out_m, out_s))
        ]

    def receive(s, j):
        half = dp >> (s + 1)
        exchange(s, j).wait_recv()
        if s < bits - 1:
            acc[j, pl.ds(0, half)] += recv[s][j]
            exchange(s + 1, j).start()
            return
        if j == 0:
            for copy in wms_copies:
                copy.wait()
        grad = acc[j, 0] + recv[s][j, 0]
        moved, new_moment, new_second = finish(
            grad, wms[0, :, cols(j)], wms[1, :, cols(j)], wms[2, :, cols(j)]
        )
        res[0, :, cols(j)] = moved
        res[1, :, cols(j)] = new_moment
        res[2, :, cols(j)] = new_second
        for copy in out_copies(j)[1:]:
            copy.start()
        square = moved * moved
        part = square[:, :128]
        for c in range(1, CHUNK // 128):
            part += square[:, c * 128 : (c + 1) * 128]
        tot[...] = part if j == 0 else tot[...] + part

    for j in range(n):
        multiply(j)
        if j == 0:
            pl.semaphore_wait(barrier, bits + nt - 1)
        exchange(0, j).start()
        if j >= 1:
            receive(0, j - 1)
    receive(0, n - 1)
    for i in range(n + LAG * (bits - 2)):
        for s in range(1, bits):
            j = i - LAG * (s - 1)
            if 0 <= j < n:
                receive(s, j)

    exact = lax.Precision.HIGHEST
    zsend[...] = lax.dot_general(
        jnp.ones((8, 128), jnp.float32),
        tot[...],
        (((1,), (1,)), ((), ())),
        precision=exact,
        preferred_element_type=jnp.float32,
    )

    def share(d):
        return pltpu.make_async_remote_copy(
            src_ref=zsend,
            dst_ref=zrecv.at[d],
            send_sem=zs_sem.at[d],
            recv_sem=zr_sem.at[d],
            device_id=(me, peers[d]),
            device_id_type=MESH,
        )

    for d in range(nt - 1):
        share(d).start()
    total = zsend[...]
    for d in range(nt - 1):
        share(d).wait_recv()
        total = total + zrecv[d]
    row_total = lax.dot_general(
        total,
        jnp.full((8, 128), 0.125, jnp.float32),
        (((0,), (0,)), ((), ())),
        precision=exact,
        preferred_element_type=jnp.float32,
    )
    scale = lax.rsqrt(row_total / (width * nt) + 1e-06)
    for c in range(width // 128):
        cs = slice(c * 128, (c + 1) * 128)
        res[0, :, cs] = res[0, :, cs] * scale
        if (c + 1) * 128 % CHUNK == 0:
            out_copies(c * 128 // CHUNK)[0].start()
    for d in range(nt - 1):
        share(d).wait_send()
    for s in range(bits):
        for j in range(n):
            exchange(s, j).wait_send()
    for j in range(n):
        for copy in out_copies(j):
            copy.wait()


def on_device(dp, nt, out_grad, inputs, weights, moment, second):
    tokens, rows = out_grad.shape
    block, width = weights.shape
    n = width // CHUNK
    bits = dp.bit_length() - 1
    dma = pltpu.SemaphoreType.DMA
    scratch = [
        pltpu.VMEM((tokens, rows), jnp.bfloat16),
        pltpu.VMEM((rows, tokens), jnp.bfloat16),
        pltpu.VMEM((SLOTS, tokens, CHUNK), jnp.bfloat16),
        pltpu.VMEM((3, block, width), jnp.float32),
        pltpu.VMEM((3, block, width), jnp.float32),
        pltpu.VMEM((n, dp, block, CHUNK), jnp.float32),
        pltpu.VMEM((block, 128), jnp.float32),
        pltpu.VMEM((8, block), jnp.float32),
        pltpu.VMEM((nt - 1, 8, block), jnp.float32),
    ]
    scratch += [
        pltpu.VMEM((n, dp >> (s + 1), block, CHUNK), jnp.float32) for s in range(bits)
    ]
    scratch += [
        dma,
        dma((SLOTS,)),
        dma((3,)),
        dma((3, n)),
        dma((bits, n)),
        dma((bits, n)),
        dma((nt - 1,)),
        dma((nt - 1,)),
    ]
    return pl.pallas_call(
        functools.partial(kernel, dp, nt),
        out_shape=[jax.ShapeDtypeStruct(weights.shape, jnp.float32)] * 3,
        in_specs=[pl.BlockSpec(memory_space=pl.ANY)] * 5,
        out_specs=[pl.BlockSpec(memory_space=pl.ANY)] * 3,
        scratch_shapes=scratch,
        compiler_params=pltpu.CompilerParams(
            collective_id=0, has_side_effects=True, vmem_limit_bytes=60 << 20
        ),
    )(out_grad, inputs, weights, moment, second)


def solution(mesh):
    held = P("dp", "tensor")
    return jax.shard_map(
        functools.partial(on_device, mesh.shape["dp"], mesh.shape["tensor"]),
        mesh=mesh,
        in_specs=(P("dp", None), held, held, held, held),
        out_specs=(held, held, held),
        check_vma=False,
    )
```

time: 94.9 us -> 43.7 us (0.46)
  waiting for transfers between devices: 54.2 us -> 0 us
  Pallas kernels: 0 us -> 37.2 us
  between operations: 14 us -> 0.64 us
  blocking collectives: 11.7 us -> 0 us
  matrix products: 9.42 us -> 0 us
  local copies, waits for them, and re-layouts: 1.55 us -> 5.61 us
  other arithmetic: 3.71 us -> 0 us
    reduce_scatter x1 -> x0, waiting for transfers between devices: 54.2 us -> none  [on_device(): lax.psum_scatter(lax.dot_general(out_grad, inputs, (((0,), (0,)), ((), ()...]
    pallas_call x0 -> x1, Pallas kernels: none -> 37.2 us  [on_device(): pl.pallas_call(functools.partial(kernel, dp, nt), out_shape=[jax.ShapeDty...]
    psum x1 -> x0, blocking collectives: 11.7 us -> none  [on_device(): totals = lax.psum(jnp.sum(moved * moved, axis=1), 'tensor')]
    dot_general x1 -> x0, matrix products: 9.42 us -> none  [on_device(): lax.dot_general(out_grad, inputs, (((0,), (0,)), ((), ())), preferred_ele...]
    unnamed x4 -> x3, local copies, waits for them, and re-layouts: 1.55 us -> 5.61 us
    reduce_sum x1 -> x0, other arithmetic: 2.79 us -> none  [on_device(): totals = lax.psum(jnp.sum(moved * moved, axis=1), 'tensor')]
  transfers between devices with their start and end apart: 1 -> 0, of which waited for: 1 -> 0; matrix products, arithmetic and copies ran while one was open for 0% -> 0% of each run, Pallas kernels for 0% -> 0%
where the time goes in v1:
time: 43.7 us; the launch traced here: 43.5 us
  Pallas kernels  37.2 us (85%)
  local copies, waits for them, and re-layouts  5.61 us (13%)
  between operations  0.64 us (1%)
    pallas_call x1, Pallas kernels, on_device(): pl.pallas_call(functools.partial(kernel, dp, nt), out_shape=[jax.ShapeDty...  37.2 us
    unnamed x3, local copies, waits for them, and re-layouts  5.61 us

profile of v1, /device:TPU:0, one launch (start us, length us, event | category | flops | bytes accessed | tf_op | source)
XLA Modules:
  0.0 43.5 jit_solution(1411787296900297278)
XLA Ops:
  0.6 37.2 %shard_map.76 = (f32[64,2048]{1,0:T(8,128)}, f32[64,2048]{1,0:T(8,128)}, f32[64,2048]{1,0:T(8,128)}) custom-call(bf16[2048,512]{1,0:T(8,128)(2,1)} %og_hbm.1, bf16[2048,2048]{1,0:T(8,128)(2,1)} %in_hbm.1, f32[64,2048]{1,0:T(8,128)} %w_hbm.1, f32[64,2048]{1,0:T(8,128)} %m_hbm.1, f32[64,2048]{1,0:T(8,128)} %s_hbm.1), custom_call_target="tpu_custom_call" | custom-call | tf_op jit(solution)/shard_map/pallas_call | solution.py:249
  37.8 1.9 %copy.11 = f32[64,2048]{1,0:T(8,128)} copy(f32[64,2048]{1,0:T(8,128)} %get-tuple-element.6) | data formatting | bytes 1048576
  39.7 1.9 %copy.12 = f32[64,2048]{1,0:T(8,128)} copy(f32[64,2048]{1,0:T(8,128)} %get-tuple-element.7) | data formatting | bytes 1048576
  41.6 1.9 %copy.13 = f32[64,2048]{1,0:T(8,128)} copy(f32[64,2048]{1,0:T(8,128)} %get-tuple-element.8) | data formatting | bytes 1048576

commit v2 on v1

--- a/solution.py
+++ b/solution.py
@@ -1,4 +1,5 @@
 import functools
+import math
 
 import jax
 import jax.numpy as jnp
@@ -30,9 +31,9 @@
     dp, nt, og_hbm, in_hbm, w_hbm, m_hbm, s_hbm, out_w, out_m, out_s, *scratch
 ):
     bits = dp.bit_length() - 1
-    og, og_t, ins, wms, res, acc, tot, zsend, zrecv = scratch[:9]
-    recv = scratch[9 : 9 + bits]
-    og_sem, in_sem, wms_sem, out_sem, send_sem, recv_sem, zs_sem, zr_sem = scratch[9 + bits :]
+    og, og_t, ins, wms, acc, tot, zsend, zrecv = scratch[:8]
+    recv = scratch[8 : 8 + bits]
+    og_sem, in_sem, wms_sem, send_sem, recv_sem, zs_sem, zr_sem = scratch[8 + bits :]
     tokens, rows = og.shape
     block = rows // dp
     width = w_hbm.shape[1]
@@ -120,14 +121,6 @@
         lax.fori_loop(0, rows // GROUP, group, 0)
         if j + SLOTS < n:
             in_copy(j + SLOTS).start()
-
-    def out_copies(j):
-        return [
-            pltpu.make_async_copy(
-                res.at[i, :, cols(j)], ref.at[:, cols(j)], out_sem.at[i, j]
-            )
-            for i, ref in enumerate((out_w, out_m, out_s))
-        ]
 
     def receive(s, j):
         half = dp >> (s + 1)
@@ -143,11 +136,9 @@
         moved, new_moment, new_second = finish(
             grad, wms[0, :, cols(j)], wms[1, :, cols(j)], wms[2, :, cols(j)]
         )
-        res[0, :, cols(j)] = moved
-        res[1, :, cols(j)] = new_moment
-        res[2, :, cols(j)] = new_second
-        for copy in out_copies(j)[1:]:
-            copy.start()
+        out_w[:, cols(j)] = moved
+        out_m[:, cols(j)] = new_moment
+        out_s[:, cols(j)] = new_second
         square = moved * moved
         part = square[:, :128]
         for c in range(1, CHUNK // 128):
@@ -203,17 +194,12 @@
     scale = lax.rsqrt(row_total / (width * nt) + 1e-06)
     for c in range(width // 128):
         cs = slice(c * 128, (c + 1) * 128)
-        res[0, :, cs] = res[0, :, cs] * scale
-        if (c + 1) * 128 % CHUNK == 0:
-            out_copies(c * 128 // CHUNK)[0].start()
+        out_w[:, cs] = out_w[:, cs] * scale
     for d in range(nt - 1):
         share(d).wait_send()
     for s in range(bits):
         for j in range(n):
             exchange(s, j).wait_send()
-    for j in range(n):
-        for copy in out_copies(j):
-            copy.wait()
 
 
 def on_device(dp, nt, out_grad, inputs, weights, moment, second):
@@ -227,7 +213,6 @@
         pltpu.VMEM((rows, tokens), jnp.bfloat16),
         pltpu.VMEM((SLOTS, tokens, CHUNK), jnp.bfloat16),
         pltpu.VMEM((3, block, width), jnp.float32),
-        pltpu.VMEM((3, block, width), jnp.float32),
         pltpu.VMEM((n, dp, block, CHUNK), jnp.float32),
         pltpu.VMEM((block, 128), jnp.float32),
         pltpu.VMEM((8, block), jnp.float32),
@@ -240,22 +225,31 @@
         dma,
         dma((SLOTS,)),
         dma((3,)),
-        dma((3, n)),
         dma((bits, n)),
         dma((bits, n)),
         dma((nt - 1,)),
         dma((nt - 1,)),
     ]
+    held = sum(
+        jnp.dtype(ref.dtype).itemsize * math.prod(ref.shape)
+        for ref in scratch
+        if getattr(ref, "memory_space", None) == pltpu.VMEM
+    )
     return pl.pallas_call(
         functools.partial(kernel, dp, nt),
-        out_shape=[jax.ShapeDtypeStruct(weights.shape, jnp.float32)] * 3,
-        in_specs=[pl.BlockSpec(memory_space=pl.ANY)] * 5,
-        out_specs=[pl.BlockSpec(memory_space=pl.ANY)] * 3,
+        out_shape=[pltpu.VMEM(weights.shape, jnp.float32)] * 3,
+        in_specs=[pl.BlockSpec(memory_space=pltpu.HBM)] * 5,
+        out_specs=[pl.BlockSpec(memory_space=pltpu.VMEM)] * 3,
         scratch_shapes=scratch,
         compiler_params=pltpu.CompilerParams(
-            collective_id=0, has_side_effects=True, vmem_limit_bytes=60 << 20
+            collective_id=0, has_side_effects=True, vmem_limit_bytes=held + (3 << 20)
         ),
-    )(out_grad, inputs, weights, moment, second)
+    )(
+        *(
+            pltpu.with_memory_space_constraint(x, pltpu.HBM)
+            for x in (out_grad, inputs, weights, moment, second)
+        )
+    )
 
 
 def solution(mesh):

time: 43.7 us -> 39.4 us (0.902)
  local copies, waits for them, and re-layouts: 5.61 us -> 2.38 us
  Pallas kernels: 37.2 us -> 36.2 us
    unnamed x3, local copies, waits for them, and re-layouts: 5.61 us -> 2.38 us
    pallas_call x1, Pallas kernels: 37.2 us -> 36.2 us  [on_device(): pl.pallas_call(functools.partial(kernel, dp, nt), out_shape=[pltpu.VMEM(w...]
where the time goes in v2:
time: 39.4 us; the launch traced here: 39.3 us
  Pallas kernels  36.2 us (92%)
  local copies, waits for them, and re-layouts  2.38 us (6%)
  between operations  0.64 us (2%)
    pallas_call x1, Pallas kernels, on_device(): pl.pallas_call(functools.partial(kernel, dp, nt), out_shape=[pltpu.VMEM(w...  36.2 us
    unnamed x3, local copies, waits for them, and re-layouts  2.38 us

profile of v2, /device:TPU:0, one launch (start us, length us, event | category | flops | bytes accessed | tf_op | source)
XLA Modules:
  0.0 39.3 jit_solution(6035753277662082865)
XLA Ops:
  0.6 36.2 %shard_map.76 = (f32[64,2048]{1,0:T(8,128)S(1)}, f32[64,2048]{1,0:T(8,128)S(1)}, f32[64,2048]{1,0:T(8,128)S(1)}) custom-call(bf16[2048,512]{1,0:T(8,128)(2,1)} %og_hbm.1, bf16[2048,2048]{1,0:T(8,128)(2,1)} %in_hbm.1, f32[64,2048]{1,0:T(8,128)} %w_hbm.1, f32[64,2048]{1,0:T(8,128)} %m_hbm.1, f32[64,2048]{1,0:T(8,128)} %s_hbm.1), custom_call_target="tpu_custom_call" | custom-call | tf_op jit(solution)/shard_map/pallas_call | solution.py:238
  36.9 0.8 %copy.11 = f32[64,2048]{1,0:T(8,128)} copy(f32[64,2048]{1,0:T(8,128)S(1)} %get-tuple-element.3) | data formatting | bytes 1048576
  37.7 0.8 %copy.12 = f32[64,2048]{1,0:T(8,128)} copy(f32[64,2048]{1,0:T(8,128)S(1)} %get-tuple-element.4) | data formatting | bytes 1048576
  38.5 0.8 %copy.13 = f32[64,2048]{1,0:T(8,128)} copy(f32[64,2048]{1,0:T(8,128)S(1)} %get-tuple-element.5) | data formatting | bytes 1048576

commit v3 on v2

--- a/solution.py
+++ b/solution.py
@@ -13,6 +13,8 @@
 SLOTS = 4
 GROUP = 512
 LAG = 3
+PIECES = 4
+SPLIT = 2
 
 
 def finish(grad, weights, moment, second):
@@ -28,7 +30,7 @@
 
 
 def kernel(
-    dp, nt, og_hbm, in_hbm, w_hbm, m_hbm, s_hbm, out_w, out_m, out_s, *scratch
+    dp, nt, og_hbm, in_hbm, w_hbm, m_hbm, s_hbm, moved_ref, moment_ref, second_ref, out_scale, *scratch
 ):
     bits = dp.bit_length() - 1
     og, og_t, ins, wms, acc, tot, zsend, zrecv = scratch[:8]
@@ -68,16 +70,19 @@
             device_id_type=MESH,
         )
 
-    og_copy = pltpu.make_async_copy(og_hbm, og, og_sem)
-    og_copy.start()
-    for j in range(min(SLOTS, n)):
-        in_copy(j).start()
+    piece = tokens // PIECES
+
+    def og_copy(p):
+        at = slice(p * piece, (p + 1) * piece)
+        return pltpu.make_async_copy(og_hbm.at[at], og.at[at], og_sem.at[p])
+
+    for p in range(PIECES):
+        og_copy(p).start()
+    in_copy(0).start()
     wms_copies = [
         pltpu.make_async_copy(ref, wms.at[i], wms_sem.at[i])
         for i, ref in enumerate((w_hbm, m_hbm, s_hbm))
     ]
-    for copy in wms_copies:
-        copy.start()
 
     barrier = pltpu.get_barrier_semaphore()
     peers = [lax.rem(z + d, nt) for d in range(1, nt)]
@@ -87,40 +92,54 @@
         pl.semaphore_signal(barrier, inc=1, device_id=(me, peer), device_id_type=MESH)
 
     tile = 256
-    eye = (
-        lax.broadcasted_iota(jnp.int32, (tile, tile), 0)
-        == lax.broadcasted_iota(jnp.int32, (tile, tile), 1)
-    ).astype(jnp.bfloat16)
-    og_copy.wait()
-
-    @pl.loop(0, rows // tile)
-    def _(r):
-        at = pl.ds(pl.multiple_of(r * tile, tile), tile)
-        for k in range(tokens // tile):
-            ks = slice(k * tile, (k + 1) * tile)
-            og_t[at, ks] = lax.dot_general(
-                eye, og[ks, at], (((1,), (1,)), ((), ())), preferred_element_type=jnp.float32
-            ).astype(jnp.bfloat16)
-
-    def multiply(j):
-        in_copy(j).wait()
-
+    place_of = lax.broadcasted_iota(jnp.int32, (tile, tile), 0)
+    row_of = lax.broadcasted_iota(jnp.int32, (tile, tile), 1)
+    own = place_of // (tile // 2)
+    pair = (place_of % (tile // 2)) // block
+    core = bit(me, 0)
+    wanted = (2 * pair + 1 - core + own * (2 * core - 1)) * block + place_of % block
+    select = (wanted == row_of).astype(jnp.bfloat16)
+    for p in range(PIECES):
+        og_copy(p).wait()
+        if p == PIECES - 1:
+            for j in range(1, min(SLOTS, n)):
+                in_copy(j).start()
+
+        def transpose(r, _, p=p):
+            rs = pl.ds(pl.multiple_of(r * tile, tile), tile)
+            for k in range(p * piece // tile, (p + 1) * piece // tile):
+                ks = slice(k * tile, (k + 1) * tile)
+                turned = lax.dot_general(
+                    select,
+                    og[ks, rs],
+                    (((1,), (1,)), ((), ())),
+                    preferred_element_type=jnp.float32,
+                ).astype(jnp.bfloat16)
+                for h in range(2):
+                    at = h * (rows // 2) + r * (tile // 2)
+                    og_t[pl.ds(pl.multiple_of(at, tile // 2), tile // 2), ks] = turned[
+                        h * (tile // 2) : (h + 1) * (tile // 2)
+                    ]
+            return 0
+
+        lax.fori_loop(0, rows // tile, transpose, 0, unroll=rows <= 2 * tile)
+
+    def multiply(j, size, first, last):
         def group(g, _):
-            at = pl.ds(pl.multiple_of(g * GROUP, GROUP), GROUP)
+            at = pl.ds(pl.multiple_of(g * size, size), size)
             part = jnp.dot(
                 og_t[at, :], ins[j % SLOTS], preferred_element_type=jnp.float32
             )
-            for o in range(GROUP // block):
-                owner = g * (GROUP // block) + o
-                place = 0
+            for o in range(size // block):
+                at = g * (size // block) + o
+                place = (1 - at // (dp // 2)) * (dp // 2)
                 for s, b in enumerate(orders[j % 2]):
-                    place += lax.rem(bit(me, b) + bit(owner, b), 2) * (dp >> (s + 1))
+                    if s:
+                        place += lax.rem(bit(me, b) + bit(at, b - 1), 2) * (dp >> (s + 1))
                 acc[j, place] = part[o * block : (o + 1) * block]
             return 0
 
-        lax.fori_loop(0, rows // GROUP, group, 0)
-        if j + SLOTS < n:
-            in_copy(j + SLOTS).start()
+        lax.fori_loop(first // size, last // size, group, 0)
 
     def receive(s, j):
         half = dp >> (s + 1)
@@ -136,9 +155,9 @@
         moved, new_moment, new_second = finish(
             grad, wms[0, :, cols(j)], wms[1, :, cols(j)], wms[2, :, cols(j)]
         )
-        out_w[:, cols(j)] = moved
-        out_m[:, cols(j)] = new_moment
-        out_s[:, cols(j)] = new_second
+        moved_ref[:, cols(j)] = moved
+        moment_ref[:, cols(j)] = new_moment
+        second_ref[:, cols(j)] = new_second
         square = moved * moved
         part = square[:, :128]
         for c in range(1, CHUNK // 128):
@@ -146,10 +165,21 @@
         tot[...] = part if j == 0 else tot[...] + part
 
     for j in range(n):
-        multiply(j)
+        in_copy(j).wait()
+        if j < SPLIT:
+            multiply(j, GROUP // 2, 0, rows // 2)
+            if j == 0:
+                pl.semaphore_wait(barrier, bits + nt - 1)
+            exchange(0, j).start()
+            multiply(j, GROUP // 2, rows // 2, rows)
+        else:
+            multiply(j, GROUP, 0, rows)
+            exchange(0, j).start()
         if j == 0:
-            pl.semaphore_wait(barrier, bits + nt - 1)
-        exchange(0, j).start()
+            for copy in wms_copies:
+                copy.start()
+        if j + SLOTS < n:
+            in_copy(j + SLOTS).start()
         if j >= 1:
             receive(0, j - 1)
     receive(0, n - 1)
@@ -191,15 +221,27 @@
         precision=exact,
         preferred_element_type=jnp.float32,
     )
-    scale = lax.rsqrt(row_total / (width * nt) + 1e-06)
-    for c in range(width // 128):
-        cs = slice(c * 128, (c + 1) * 128)
-        out_w[:, cs] = out_w[:, cs] * scale
+    out_scale[...] = lax.rsqrt(row_total / (width * nt) + 1e-06)
     for d in range(nt - 1):
         share(d).wait_send()
     for s in range(bits):
         for j in range(n):
             exchange(s, j).wait_send()
+
+
+def write_kernel(moved, moment, second, scale, out_w, out_m, out_s, scaled, sem):
+    copies = [
+        pltpu.make_async_copy(src, dst, sem.at[i])
+        for i, (src, dst) in enumerate(((scaled, out_w), (moment, out_m), (second, out_s)))
+    ]
+    copies[1].start()
+    copies[2].start()
+    for c in range(moved.shape[1] // 128):
+        cs = slice(c * 128, (c + 1) * 128)
+        scaled[:, cs] = moved[:, cs] * scale[...]
+    copies[0].start()
+    for copy in copies:
+        copy.wait()
 
 
 def on_device(dp, nt, out_grad, inputs, weights, moment, second):
@@ -222,7 +264,7 @@
         pltpu.VMEM((n, dp >> (s + 1), block, CHUNK), jnp.float32) for s in range(bits)
     ]
     scratch += [
-        dma,
+        dma((PIECES,)),
         dma((SLOTS,)),
         dma((3,)),
         dma((bits, n)),
@@ -235,11 +277,12 @@
         for ref in scratch
         if getattr(ref, "memory_space", None) == pltpu.VMEM
     )
-    return pl.pallas_call(
+    shapes = [weights.shape] * 3 + [(block, 128)]
+    results = pl.pallas_call(
         functools.partial(kernel, dp, nt),
-        out_shape=[pltpu.VMEM(weights.shape, jnp.float32)] * 3,
+        out_shape=[pltpu.VMEM(shape, jnp.float32) for shape in shapes],
         in_specs=[pl.BlockSpec(memory_space=pltpu.HBM)] * 5,
-        out_specs=[pl.BlockSpec(memory_space=pltpu.VMEM)] * 3,
+        out_specs=[pl.BlockSpec(memory_space=pltpu.VMEM)] * 4,
         scratch_shapes=scratch,
         compiler_params=pltpu.CompilerParams(
             collective_id=0, has_side_effects=True, vmem_limit_bytes=held + (3 << 20)
@@ -250,6 +293,14 @@
             for x in (out_grad, inputs, weights, moment, second)
         )
     )
+    return pl.pallas_call(
+        write_kernel,
+        out_shape=[pltpu.HBM(weights.shape, jnp.float32)] * 3,
+        in_specs=[pl.BlockSpec(memory_space=pltpu.VMEM)] * 4,
+        out_specs=[pl.BlockSpec(memory_space=pltpu.HBM)] * 3,
+        scratch_shapes=[pltpu.VMEM(weights.shape, jnp.float32), dma((3,))],
+        compiler_params=pltpu.CompilerParams(vmem_limit_bytes=2 << 20),
+    )(*results)
 
 
 def solution(mesh):

time: 39.4 us -> 36.7 us (0.931)
  local copies, waits for them, and re-layouts: 2.38 us -> 0 us
    unnamed x3 -> x0, local copies, waits for them, and re-layouts: 2.38 us -> none
    pallas_call x1 -> x2, Pallas kernels: 36.2 us -> 35.9 us  [the longest x1 34.7 us: on_device(): pl.pallas_call(functools.partial(kernel, dp, nt), out_shape=[pltpu.VMEM(s...]
where the time goes in v3:
time: 36.7 us; the launch traced here: 36.5 us
  Pallas kernels  35.9 us (98%)
  between operations  0.64 us (2%)
    pallas_call x1, Pallas kernels, on_device(): pl.pallas_call(functools.partial(kernel, dp, nt), out_shape=[pltpu.VMEM(s...  34.7 us
    pallas_call x1, Pallas kernels, on_device(): pl.pallas_call(write_kernel, out_shape=[pltpu.HBM(weights.shape, jnp.floa...  1.17 us

profile of v3, /device:TPU:0, one launch (start us, length us, event | category | flops | bytes accessed | tf_op | source)
XLA Modules:
  0.0 36.5 jit_solution(6781797088508323759)
XLA Ops:
  0.6 34.7 %shard_map.76 = (f32[64,2048]{1,0:T(8,128)S(1)}, f32[64,2048]{1,0:T(8,128)S(1)}, f32[64,2048]{1,0:T(8,128)S(1)}, f32[64,128]{1,0:T(8,128)S(1)}) custom-call(bf16[2048,512]{1,0:T(8,128)(2,1)} %og_hbm.1, bf16[2048,2048]{1,0:T(8,128)(2,1)} %in_hbm.1, f32[64,2048]{1,0:T(8,128)} %w_hbm.1, f32[64,2048]{1,0:T(8,128)} %m_hbm.1, f32[64,2048]{1,0:T(8,128)} %s_hbm.1), custom_call_target="tpu_custom_call" | custom-call | tf_op jit(solution)/shard_map/pallas_call | solution.py:281
  35.3 1.2 %shard_map.77 = (f32[64,2048]{1,0:T(8,128)}, f32[64,2048]{1,0:T(8,128)}, f32[64,2048]{1,0:T(8,128)}) custom-call(f32[64,2048]{1,0:T(8,128)S(1)} %get-tuple-element.7.moved, f32[64,2048]{1,0:T(8,128)S(1)} %get-tuple-element.8.moment, f32[64,2048]{1,0:T(8,128)S(1)} %get-tuple-element.9.second, f32[64,128]{1,0:T(8,128)S(1)} %get-tuple-element.10.scale), custom_call_target="tpu_custom_call" | custom-call | tf_op jit(solution)/shard_map/pallas_call | solution.py:296

commit v4 on v3

--- a/solution.py
+++ b/solution.py
@@ -10,9 +10,10 @@
 
 MESH = pl.DeviceIdType.MESH
 CHUNK = 256
+PART = 128
 SLOTS = 4
 GROUP = 512
-LAG = 3
+LAG = 6
 PIECES = 4
 SPLIT = 2
 
@@ -39,7 +40,8 @@
     tokens, rows = og.shape
     block = rows // dp
     width = w_hbm.shape[1]
-    n = width // CHUNK
+    n, parts = width // CHUNK, width // PART
+    share_of = CHUNK // PART
     me, z = lax.axis_index("dp"), lax.axis_index("tensor")
 
     plane = (bits - 1) // 2
@@ -51,12 +53,12 @@
         mine = bit(me, b)
         return (me + (1 - 2 * mine) * (1 << b), z)
 
-    def cols(j):
-        return slice(j * CHUNK, (j + 1) * CHUNK)
+    def cols(j, size=PART):
+        return slice(j * size, (j + 1) * size)
 
     def in_copy(j):
         return pltpu.make_async_copy(
-            in_hbm.at[:, cols(j)], ins.at[j % SLOTS], in_sem.at[j % SLOTS]
+            in_hbm.at[:, cols(j, CHUNK)], ins.at[j % SLOTS], in_sem.at[j % SLOTS]
         )
 
     def exchange(s, j):
@@ -132,11 +134,12 @@
             )
             for o in range(size // block):
                 at = g * (size // block) + o
-                place = (1 - at // (dp // 2)) * (dp // 2)
-                for s, b in enumerate(orders[j % 2]):
-                    if s:
-                        place += lax.rem(bit(me, b) + bit(at, b - 1), 2) * (dp >> (s + 1))
-                acc[j, place] = part[o * block : (o + 1) * block]
+                for q in range(share_of):
+                    place = (1 - at // (dp // 2)) * (dp // 2)
+                    for s, b in enumerate(orders[q % 2]):
+                        if s:
+                            place += lax.rem(bit(me, b) + bit(at, b - 1), 2) * (dp >> (s + 1))
+                    acc[j * share_of + q, place] = part[o * block : (o + 1) * block, cols(q)]
             return 0
 
         lax.fori_loop(first // size, last // size, group, 0)
@@ -159,10 +162,11 @@
         moment_ref[:, cols(j)] = new_moment
         second_ref[:, cols(j)] = new_second
         square = moved * moved
-        part = square[:, :128]
-        for c in range(1, CHUNK // 128):
-            part += square[:, c * 128 : (c + 1) * 128]
-        tot[...] = part if j == 0 else tot[...] + part
+        tot[...] = square if j == 0 else tot[...] + square
+
+    def each(j, action):
+        for q in range(share_of):
+            action(j * share_of + q)
 
     for j in range(n):
         in_copy(j).wait()
@@ -170,23 +174,23 @@
             multiply(j, GROUP // 2, 0, rows // 2)
             if j == 0:
                 pl.semaphore_wait(barrier, bits + nt - 1)
-            exchange(0, j).start()
+            each(j, lambda q: exchange(0, q).start())
             multiply(j, GROUP // 2, rows // 2, rows)
         else:
             multiply(j, GROUP, 0, rows)
-            exchange(0, j).start()
+            each(j, lambda q: exchange(0, q).start())
         if j == 0:
             for copy in wms_copies:
                 copy.start()
         if j + SLOTS < n:
             in_copy(j + SLOTS).start()
         if j >= 1:
-            receive(0, j - 1)
-    receive(0, n - 1)
-    for i in range(n + LAG * (bits - 2)):
+            each(j - 1, lambda q: receive(0, q))
+    each(n - 1, lambda q: receive(0, q))
+    for i in range(parts + LAG * (bits - 2)):
         for s in range(1, bits):
             j = i - LAG * (s - 1)
-            if 0 <= j < n:
+            if 0 <= j < parts:
                 receive(s, j)
 
     exact = lax.Precision.HIGHEST
@@ -210,6 +214,11 @@
 
     for d in range(nt - 1):
         share(d).start()
+    for s in range(bits):
+        for j in range(parts):
+            exchange(s, j).wait_send()
+    for d in range(nt - 1):
+        share(d).wait_send()
     total = zsend[...]
     for d in range(nt - 1):
         share(d).wait_recv()
@@ -222,11 +231,6 @@
         preferred_element_type=jnp.float32,
     )
     out_scale[...] = lax.rsqrt(row_total / (width * nt) + 1e-06)
-    for d in range(nt - 1):
-        share(d).wait_send()
-    for s in range(bits):
-        for j in range(n):
-            exchange(s, j).wait_send()
 
 
 def write_kernel(moved, moment, second, scale, out_w, out_m, out_s, scaled, sem):
@@ -247,7 +251,7 @@
 def on_device(dp, nt, out_grad, inputs, weights, moment, second):
     tokens, rows = out_grad.shape
     block, width = weights.shape
-    n = width // CHUNK
+    parts = width // PART
     bits = dp.bit_length() - 1
     dma = pltpu.SemaphoreType.DMA
     scratch = [
@@ -255,20 +259,20 @@
         pltpu.VMEM((rows, tokens), jnp.bfloat16),
         pltpu.VMEM((SLOTS, tokens, CHUNK), jnp.bfloat16),
         pltpu.VMEM((3, block, width), jnp.float32),
-        pltpu.VMEM((n, dp, block, CHUNK), jnp.float32),
+        pltpu.VMEM((parts, dp, block, PART), jnp.float32),
         pltpu.VMEM((block, 128), jnp.float32),
         pltpu.VMEM((8, block), jnp.float32),
         pltpu.VMEM((nt - 1, 8, block), jnp.float32),
     ]
     scratch += [
-        pltpu.VMEM((n, dp >> (s + 1), block, CHUNK), jnp.float32) for s in range(bits)
+        pltpu.VMEM((parts, dp >> (s + 1), block, PART), jnp.float32) for s in range(bits)
     ]
     scratch += [
         dma((PIECES,)),
         dma((SLOTS,)),
         dma((3,)),
-        dma((bits, n)),
-        dma((bits, n)),
+        dma((bits, parts)),
+        dma((bits, parts)),
         dma((nt - 1,)),
         dma((nt - 1,)),
     ]

time: 36.7 us -> 36.2 us (0.986)
  Pallas kernels: 35.9 us -> 35.4 us
    pallas_call x1, Pallas kernels: 34.7 us -> 34.2 us  [on_device(): pl.pallas_call(functools.partial(kernel, dp, nt), out_shape=[pltpu.VMEM(s...]
where the time goes in v4:
time: 36.2 us; the launch traced here: 36 us
  Pallas kernels  35.4 us (98%)
  between operations  0.64 us (2%)
    pallas_call x1, Pallas kernels, on_device(): pl.pallas_call(functools.partial(kernel, dp, nt), out_shape=[pltpu.VMEM(s...  34.2 us
    pallas_call x1, Pallas kernels, on_device(): pl.pallas_call(write_kernel, out_shape=[pltpu.HBM(weights.shape, jnp.floa...  1.17 us

profile of v4, /device:TPU:0, one launch (start us, length us, event | category | flops | bytes accessed | tf_op | source)
XLA Modules:
  0.0 36.0 jit_solution(8627261125677809528)
XLA Ops:
  0.6 34.2 %shard_map.76 = (f32[64,2048]{1,0:T(8,128)S(1)}, f32[64,2048]{1,0:T(8,128)S(1)}, f32[64,2048]{1,0:T(8,128)S(1)}, f32[64,128]{1,0:T(8,128)S(1)}) custom-call(bf16[2048,512]{1,0:T(8,128)(2,1)} %og_hbm.1, bf16[2048,2048]{1,0:T(8,128)(2,1)} %in_hbm.1, f32[64,2048]{1,0:T(8,128)} %w_hbm.1, f32[64,2048]{1,0:T(8,128)} %m_hbm.1, f32[64,2048]{1,0:T(8,128)} %s_hbm.1), custom_call_target="tpu_custom_call" | custom-call | tf_op jit(solution)/shard_map/pallas_call | solution.py:285
  34.8 1.2 %shard_map.77 = (f32[64,2048]{1,0:T(8,128)}, f32[64,2048]{1,0:T(8,128)}, f32[64,2048]{1,0:T(8,128)}) custom-call(f32[64,2048]{1,0:T(8,128)S(1)} %get-tuple-element.7.moved, f32[64,2048]{1,0:T(8,128)S(1)} %get-tuple-element.8.moment, f32[64,2048]{1,0:T(8,128)S(1)} %get-tuple-element.9.second, f32[64,128]{1,0:T(8,128)S(1)} %get-tuple-element.10.scale), custom_call_target="tpu_custom_call" | custom-call | tf_op jit(solution)/shard_map/pallas_call | solution.py:300

commit v5 on v4

--- a/solution.py
+++ b/solution.py
@@ -13,7 +13,6 @@
 PART = 128
 SLOTS = 4
 GROUP = 512
-LAG = 6
 PIECES = 4
 SPLIT = 2
 
@@ -175,23 +174,22 @@
             if j == 0:
                 pl.semaphore_wait(barrier, bits + nt - 1)
             each(j, lambda q: exchange(0, q).start())
+            if j:
+                each(j - 1, lambda q: receive(0, q))
             multiply(j, GROUP // 2, rows // 2, rows)
         else:
             multiply(j, GROUP, 0, rows)
             each(j, lambda q: exchange(0, q).start())
+            each(j - 1, lambda q: receive(0, q))
         if j == 0:
             for copy in wms_copies:
                 copy.start()
         if j + SLOTS < n:
             in_copy(j + SLOTS).start()
-        if j >= 1:
-            each(j - 1, lambda q: receive(0, q))
     each(n - 1, lambda q: receive(0, q))
-    for i in range(parts + LAG * (bits - 2)):
-        for s in range(1, bits):
-            j = i - LAG * (s - 1)
-            if 0 <= j < parts:
-                receive(s, j)
+    for s in range(1, bits):
+        for j in range(parts):
+            receive(s, j)
 
     exact = lax.Precision.HIGHEST
     zsend[...] = lax.dot_general(

time: 36.2 us -> 34.5 us (0.953)
  Pallas kernels: 35.4 us -> 33.7 us
    pallas_call x1, Pallas kernels: 34.2 us -> 32.6 us  [on_device(): pl.pallas_call(functools.partial(kernel, dp, nt), out_shape=[pltpu.VMEM(s...]
where the time goes in v5:
time: 34.5 us; the launch traced here: 34.4 us
  Pallas kernels  33.7 us (98%)
  between operations  0.64 us (2%)
    pallas_call x1, Pallas kernels, on_device(): pl.pallas_call(functools.partial(kernel, dp, nt), out_shape=[pltpu.VMEM(s...  32.6 us
    pallas_call x1, Pallas kernels, on_device(): pl.pallas_call(write_kernel, out_shape=[pltpu.HBM(weights.shape, jnp.floa...  1.17 us

profile of v5, /device:TPU:0, one launch (start us, length us, event | category | flops | bytes accessed | tf_op | source)
XLA Modules:
  0.0 34.4 jit_solution(18335838453692567571)
XLA Ops:
  0.6 32.6 %shard_map.76 = (f32[64,2048]{1,0:T(8,128)S(1)}, f32[64,2048]{1,0:T(8,128)S(1)}, f32[64,2048]{1,0:T(8,128)S(1)}, f32[64,128]{1,0:T(8,128)S(1)}) custom-call(bf16[2048,512]{1,0:T(8,128)(2,1)} %og_hbm.1, bf16[2048,2048]{1,0:T(8,128)(2,1)} %in_hbm.1, f32[64,2048]{1,0:T(8,128)} %w_hbm.1, f32[64,2048]{1,0:T(8,128)} %m_hbm.1, f32[64,2048]{1,0:T(8,128)} %s_hbm.1), custom_call_target="tpu_custom_call" | custom-call | tf_op jit(solution)/shard_map/pallas_call | solution.py:283
  33.2 1.2 %shard_map.77 = (f32[64,2048]{1,0:T(8,128)}, f32[64,2048]{1,0:T(8,128)}, f32[64,2048]{1,0:T(8,128)}) custom-call(f32[64,2048]{1,0:T(8,128)S(1)} %get-tuple-element.7.moved, f32[64,2048]{1,0:T(8,128)S(1)} %get-tuple-element.8.moment, f32[64,2048]{1,0:T(8,128)S(1)} %get-tuple-element.9.second, f32[64,128]{1,0:T(8,128)S(1)} %get-tuple-element.10.scale), custom_call_target="tpu_custom_call" | custom-call | tf_op jit(solution)/shard_map/pallas_call | solution.py:298

commit v6 on v5

--- a/solution.py
+++ b/solution.py
@@ -14,6 +14,7 @@
 SLOTS = 4
 GROUP = 512
 PIECES = 4
+AHEAD = 5
 SPLIT = 2
 
 
@@ -181,6 +182,8 @@
             multiply(j, GROUP, 0, rows)
             each(j, lambda q: exchange(0, q).start())
             each(j - 1, lambda q: receive(0, q))
+        if j >= AHEAD:
+            each(j - AHEAD, lambda q: receive(1, q))
         if j == 0:
             for copy in wms_copies:
                 copy.start()
@@ -188,15 +191,18 @@
             in_copy(j + SLOTS).start()
     each(n - 1, lambda q: receive(0, q))
     for s in range(1, bits):
-        for j in range(parts):
+        for j in range(max(n - AHEAD, 0) * share_of if s == 1 else 0, parts):
             receive(s, j)
 
-    exact = lax.Precision.HIGHEST
+    def pair_of(value, axis):
+        high = value.astype(jnp.bfloat16)
+        rest = (value - high.astype(jnp.float32)).astype(jnp.bfloat16)
+        return jnp.concatenate([high, rest], axis=axis)
+
     zsend[...] = lax.dot_general(
-        jnp.ones((8, 128), jnp.float32),
-        tot[...],
+        jnp.ones((8, 256), jnp.bfloat16),
+        pair_of(tot[...], 1),
         (((1,), (1,)), ((), ())),
-        precision=exact,
         preferred_element_type=jnp.float32,
     )
 
@@ -222,10 +228,9 @@
         share(d).wait_recv()
         total = total + zrecv[d]
     row_total = lax.dot_general(
-        total,
-        jnp.full((8, 128), 0.125, jnp.float32),
+        pair_of(total, 0),
+        jnp.full((16, 128), 0.125, jnp.bfloat16),
         (((0,), (0,)), ((), ())),
-        precision=exact,
         preferred_element_type=jnp.float32,
     )
     out_scale[...] = lax.rsqrt(row_total / (width * nt) + 1e-06)

time: 34.5 us -> 34.5 us (level)
  no operation moved by 1% of the time
where the time goes in v6:
time: 34.5 us; the launch traced here: 34.4 us
  Pallas kernels  33.7 us (98%)
  between operations  0.64 us (2%)
    pallas_call x1, Pallas kernels, on_device(): pl.pallas_call(functools.partial(kernel, dp, nt), out_shape=[pltpu.VMEM(s...  32.6 us
    pallas_call x1, Pallas kernels, on_device(): pl.pallas_call(write_kernel, out_shape=[pltpu.HBM(weights.shape, jnp.floa...  1.17 us

profile of v6, /device:TPU:0, one launch (start us, length us, event | category | flops | bytes accessed | tf_op | source)
XLA Modules:
  0.0 34.4 jit_solution(6433755958234237404)
XLA Ops:
  0.6 32.6 %shard_map.76 = (f32[64,2048]{1,0:T(8,128)S(1)}, f32[64,2048]{1,0:T(8,128)S(1)}, f32[64,2048]{1,0:T(8,128)S(1)}, f32[64,128]{1,0:T(8,128)S(1)}) custom-call(bf16[2048,512]{1,0:T(8,128)(2,1)} %og_hbm.1, bf16[2048,2048]{1,0:T(8,128)(2,1)} %in_hbm.1, f32[64,2048]{1,0:T(8,128)} %w_hbm.1, f32[64,2048]{1,0:T(8,128)} %m_hbm.1, f32[64,2048]{1,0:T(8,128)} %s_hbm.1), custom_call_target="tpu_custom_call" | custom-call | tf_op jit(solution)/shard_map/pallas_call | solution.py:288
  33.2 1.2 %shard_map.77 = (f32[64,2048]{1,0:T(8,128)}, f32[64,2048]{1,0:T(8,128)}, f32[64,2048]{1,0:T(8,128)}) custom-call(f32[64,2048]{1,0:T(8,128)S(1)} %get-tuple-element.7.moved, f32[64,2048]{1,0:T(8,128)S(1)} %get-tuple-element.8.moment, f32[64,2048]{1,0:T(8,128)S(1)} %get-tuple-element.9.second, f32[64,128]{1,0:T(8,128)S(1)} %get-tuple-element.10.scale), custom_call_target="tpu_custom_call" | custom-call | tf_op jit(solution)/shard_map/pallas_call | solution.py:303

commit v7 on v6

--- a/solution.py
+++ b/solution.py
@@ -61,10 +61,20 @@
             in_hbm.at[:, cols(j, CHUNK)], ins.at[j % SLOTS], in_sem.at[j % SLOTS]
         )
 
+    def swap(j):
+        return pltpu.make_async_remote_copy(
+            src_ref=acc.at[j, 1],
+            dst_ref=recv[0].at[j],
+            send_sem=send_sem.at[0, j],
+            recv_sem=recv_sem.at[0, j],
+            device_id=partner(0),
+            device_id_type=MESH,
+        )
+
     def exchange(s, j):
         half = dp >> (s + 1)
         return pltpu.make_async_remote_copy(
-            src_ref=acc.at[j, pl.ds(half, half)],
+            src_ref=acc.at[j // share_of, 0, j % share_of, pl.ds(half, half)],
             dst_ref=recv[s].at[j],
             send_sem=send_sem.at[s, j],
             recv_sem=recv_sem.at[s, j],
@@ -111,6 +121,15 @@
             rs = pl.ds(pl.multiple_of(r * tile, tile), tile)
             for k in range(p * piece // tile, (p + 1) * piece // tile):
                 ks = slice(k * tile, (k + 1) * tile)
+                if k % 2:
+                    turned = jnp.transpose(og[ks, rs])
+                    for o in range(tile // block):
+                        h = 1 - lax.rem(core + o, 2)
+                        at = h * (rows // 2) + r * (tile // 2) + (o // 2) * block
+                        og_t[pl.ds(pl.multiple_of(at, block), block), ks] = turned[
+                            o * block : (o + 1) * block
+                        ]
+                    continue
                 turned = lax.dot_general(
                     select,
                     og[ks, rs],
@@ -135,26 +154,27 @@
             for o in range(size // block):
                 at = g * (size // block) + o
                 for q in range(share_of):
-                    place = (1 - at // (dp // 2)) * (dp // 2)
+                    place = 0
                     for s, b in enumerate(orders[q % 2]):
                         if s:
                             place += lax.rem(bit(me, b) + bit(at, b - 1), 2) * (dp >> (s + 1))
-                    acc[j * share_of + q, place] = part[o * block : (o + 1) * block, cols(q)]
+                    acc[j, 1 - at // (dp // 2), q, place] = part[o * block : (o + 1) * block, cols(q)]
             return 0
 
         lax.fori_loop(first // size, last // size, group, 0)
 
     def receive(s, j):
         half = dp >> (s + 1)
+        held = (j // share_of, 0, j % share_of)
         exchange(s, j).wait_recv()
         if s < bits - 1:
-            acc[j, pl.ds(0, half)] += recv[s][j]
+            acc[(*held, pl.ds(0, half))] += recv[s][j]
             exchange(s + 1, j).start()
             return
         if j == 0:
             for copy in wms_copies:
                 copy.wait()
-        grad = acc[j, 0] + recv[s][j, 0]
+        grad = acc[(*held, 0)] + recv[s][j, 0]
         moved, new_moment, new_second = finish(
             grad, wms[0, :, cols(j)], wms[1, :, cols(j)], wms[2, :, cols(j)]
         )
@@ -163,6 +183,12 @@
         second_ref[:, cols(j)] = new_second
         square = moved * moved
         tot[...] = square if j == 0 else tot[...] + square
+
+    def sum_cores(j):
+        swap(j).wait_recv()
+        for q in range(share_of):
+            acc[j, 0, q] += recv[0][j, q]
+            exchange(1, j * share_of + q).start()
 
     def each(j, action):
         for q in range(share_of):
@@ -174,14 +200,14 @@
             multiply(j, GROUP // 2, 0, rows // 2)
             if j == 0:
                 pl.semaphore_wait(barrier, bits + nt - 1)
-            each(j, lambda q: exchange(0, q).start())
+            swap(j).start()
             if j:
-                each(j - 1, lambda q: receive(0, q))
+                sum_cores(j - 1)
             multiply(j, GROUP // 2, rows // 2, rows)
         else:
             multiply(j, GROUP, 0, rows)
-            each(j, lambda q: exchange(0, q).start())
-            each(j - 1, lambda q: receive(0, q))
+            swap(j).start()
+            sum_cores(j - 1)
         if j >= AHEAD:
             each(j - AHEAD, lambda q: receive(1, q))
         if j == 0:
@@ -189,7 +215,7 @@
                 copy.start()
         if j + SLOTS < n:
             in_copy(j + SLOTS).start()
-    each(n - 1, lambda q: receive(0, q))
+    sum_cores(n - 1)
     for s in range(1, bits):
         for j in range(max(n - AHEAD, 0) * share_of if s == 1 else 0, parts):
             receive(s, j)
@@ -218,7 +244,9 @@
 
     for d in range(nt - 1):
         share(d).start()
-    for s in range(bits):
+    for j in range(n):
+        swap(j).wait_send()
+    for s in range(1, bits):
         for j in range(parts):
             exchange(s, j).wait_send()
     for d in range(nt - 1):
@@ -262,13 +290,16 @@
         pltpu.VMEM((rows, tokens), jnp.bfloat16),
         pltpu.VMEM((SLOTS, tokens, CHUNK), jnp.bfloat16),
         pltpu.VMEM((3, block, width), jnp.float32),
-        pltpu.VMEM((parts, dp, block, PART), jnp.float32),
+        pltpu.VMEM((width // CHUNK, 2, CHUNK // PART, dp // 2, block, PART), jnp.float32),
         pltpu.VMEM((block, 128), jnp.float32),
         pltpu.VMEM((8, block), jnp.float32),
         pltpu.VMEM((nt - 1, 8, block), jnp.float32),
     ]
     scratch += [
-        pltpu.VMEM((parts, dp >> (s + 1), block, PART), jnp.float32) for s in range(bits)
+        pltpu.VMEM((width // CHUNK, CHUNK // PART, dp // 2, block, PART), jnp.float32)
+    ]
+    scratch += [
+        pltpu.VMEM((parts, dp >> (s + 1), block, PART), jnp.float32) for s in range(1, bits)
     ]
     scratch += [
         dma((PIECES,)),

time: 34.5 us -> 34.3 us (level)
  no operation moved by 1% of the time
where the time goes in v7:
time: 34.3 us; the launch traced here: 34.1 us
  Pallas kernels  33.5 us (98%)
  between operations  0.64 us (2%)
    pallas_call x1, Pallas kernels, on_device(): pl.pallas_call(functools.partial(kernel, dp, nt), out_shape=[pltpu.VMEM(s...  32.3 us
    pallas_call x1, Pallas kernels, on_device(): pl.pallas_call(write_kernel, out_shape=[pltpu.HBM(weights.shape, jnp.floa...  1.17 us

profile of v7, /device:TPU:0, one launch (start us, length us, event | category | flops | bytes accessed | tf_op | source)
XLA Modules:
  0.0 34.1 jit_solution(13826661805364110416)
XLA Ops:
  0.6 32.3 %shard_map.76 = (f32[64,2048]{1,0:T(8,128)S(1)}, f32[64,2048]{1,0:T(8,128)S(1)}, f32[64,2048]{1,0:T(8,128)S(1)}, f32[64,128]{1,0:T(8,128)S(1)}) custom-call(bf16[2048,512]{1,0:T(8,128)(2,1)} %og_hbm.1, bf16[2048,2048]{1,0:T(8,128)(2,1)} %in_hbm.1, f32[64,2048]{1,0:T(8,128)} %w_hbm.1, f32[64,2048]{1,0:T(8,128)} %m_hbm.1, f32[64,2048]{1,0:T(8,128)} %s_hbm.1), custom_call_target="tpu_custom_call" | custom-call | tf_op jit(solution)/shard_map/pallas_call | solution.py:319
  32.9 1.2 %shard_map.77 = (f32[64,2048]{1,0:T(8,128)}, f32[64,2048]{1,0:T(8,128)}, f32[64,2048]{1,0:T(8,128)}) custom-call(f32[64,2048]{1,0:T(8,128)S(1)} %get-tuple-element.7.moved, f32[64,2048]{1,0:T(8,128)S(1)} %get-tuple-element.8.moment, f32[64,2048]{1,0:T(8,128)S(1)} %get-tuple-element.9.second, f32[64,128]{1,0:T(8,128)S(1)} %get-tuple-element.10.scale), custom_call_target="tpu_custom_call" | custom-call | tf_op jit(solution)/shard_map/pallas_call | solution.py:334

commit v8 on v7

--- a/solution.py
+++ b/solution.py
@@ -43,6 +43,7 @@
     n, parts = width // CHUNK, width // PART
     share_of = CHUNK // PART
     me, z = lax.axis_index("dp"), lax.axis_index("tensor")
+    core = bit(me, 0)
 
     plane = (bits - 1) // 2
     along_x = list(range(1, 1 + plane))
@@ -60,6 +61,9 @@
         return pltpu.make_async_copy(
             in_hbm.at[:, cols(j, CHUNK)], ins.at[j % SLOTS], in_sem.at[j % SLOTS]
         )
+
+    def chosen(j, core, pair):
+        return pair[0] + lax.rem(j % 2 + core, 2) * (pair[1] - pair[0])
 
     def swap(j):
         return pltpu.make_async_remote_copy(
@@ -78,7 +82,7 @@
             dst_ref=recv[s].at[j],
             send_sem=send_sem.at[s, j],
             recv_sem=recv_sem.at[s, j],
-            device_id=partner(orders[j % 2][s]),
+            device_id=(chosen(j, core, [partner(order[s])[0] for order in orders]), z),
             device_id_type=MESH,
         )
 
@@ -108,7 +112,6 @@
     row_of = lax.broadcasted_iota(jnp.int32, (tile, tile), 1)
     own = place_of // (tile // 2)
     pair = (place_of % (tile // 2)) // block
-    core = bit(me, 0)
     wanted = (2 * pair + 1 - core + own * (2 * core - 1)) * block + place_of % block
     select = (wanted == row_of).astype(jnp.bfloat16)
     for p in range(PIECES):
@@ -154,11 +157,17 @@
             for o in range(size // block):
                 at = g * (size // block) + o
                 for q in range(share_of):
-                    place = 0
-                    for s, b in enumerate(orders[q % 2]):
-                        if s:
-                            place += lax.rem(bit(me, b) + bit(at, b - 1), 2) * (dp >> (s + 1))
-                    acc[j, 1 - at // (dp // 2), q, place] = part[o * block : (o + 1) * block, cols(q)]
+                    own = at // (dp // 2)
+                    places = [
+                        sum(
+                            lax.rem(bit(me, b) + bit(at, b - 1), 2) * (dp >> (s + 1))
+                            for s, b in enumerate(order)
+                            if s
+                        )
+                        for order in orders
+                    ]
+                    place = chosen(q, own * core + (1 - own) * (1 - core), places)
+                    acc[j, 1 - own, q, place] = part[o * block : (o + 1) * block, cols(q)]
             return 0
 
         lax.fori_loop(first // size, last // size, group, 0)

time: 34.3 us -> 34.3 us (level)
  no operation moved by 1% of the time
where the time goes in v8:
time: 34.3 us; the launch traced here: 34.1 us
  Pallas kernels  33.5 us (98%)
  between operations  0.64 us (2%)
    pallas_call x1, Pallas kernels, on_device(): pl.pallas_call(functools.partial(kernel, dp, nt), out_shape=[pltpu.VMEM(s...  32.3 us
    pallas_call x1, Pallas kernels, on_device(): pl.pallas_call(write_kernel, out_shape=[pltpu.HBM(weights.shape, jnp.floa...  1.17 us

profile of v8, /device:TPU:0, one launch (start us, length us, event | category | flops | bytes accessed | tf_op | source)
XLA Modules:
  0.0 34.1 jit_solution(819012329299672058)
XLA Ops:
  0.6 32.3 %shard_map.76 = (f32[64,2048]{1,0:T(8,128)S(1)}, f32[64,2048]{1,0:T(8,128)S(1)}, f32[64,2048]{1,0:T(8,128)S(1)}, f32[64,128]{1,0:T(8,128)S(1)}) custom-call(bf16[2048,512]{1,0:T(8,128)(2,1)} %og_hbm.1, bf16[2048,2048]{1,0:T(8,128)(2,1)} %in_hbm.1, f32[64,2048]{1,0:T(8,128)} %w_hbm.1, f32[64,2048]{1,0:T(8,128)} %m_hbm.1, f32[64,2048]{1,0:T(8,128)} %s_hbm.1), custom_call_target="tpu_custom_call" | custom-call | tf_op jit(solution)/shard_map/pallas_call | solution.py:328
  33.0 1.2 %shard_map.77 = (f32[64,2048]{1,0:T(8,128)}, f32[64,2048]{1,0:T(8,128)}, f32[64,2048]{1,0:T(8,128)}) custom-call(f32[64,2048]{1,0:T(8,128)S(1)} %get-tuple-element.7.moved, f32[64,2048]{1,0:T(8,128)S(1)} %get-tuple-element.8.moment, f32[64,2048]{1,0:T(8,128)S(1)} %get-tuple-element.9.second, f32[64,128]{1,0:T(8,128)S(1)} %get-tuple-element.10.scale), custom_call_target="tpu_custom_call" | custom-call | tf_op jit(solution)/shard_map/pallas_call | solution.py:343
